TPU v7x, 512 devices: a whole 4x4x16 slice. The times are simulated.
512 devices in a mesh: row: 16 (over z), col: 32 (over y, x, core).
Axes of the slice: x: 4, y: 4, z: 16, core: 2. Of those that a mesh axis runs over, the one named last changes fastest.
Arguments:
- points: float32 [16384, 128], P('row'), may hold values from -6 to 6
- panel_pool: float32 [16384, 128], P('col'), may hold values from -6 to 6
- order: int32 [512], replicated, may hold values from 0 to 511, each once
- panel_index: int32 [1], replicated, may hold values from 0 to 31
- inv_factor: float32 [512, 512], replicated, as said below
- ard_weights: float32 [128], replicated, may hold values from 0.001 to 0.1
- noise: float32 [16384], P('row'), may hold values from 0.05 to 1
Outputs:
- schur: float32 [16384, 16384], P('row', 'col')
Inputs may be any that keep to these rules, and one draw needn't show every extreme that they name: `order`: a permutation of 0 to 511. `inv_factor`: lower triangular: zero above the diagonal.
All inputs are finite; a program needn't handle non-finite values.
Results may differ from a plain program's by a relative error of at most 0.0003.
Values sent between devices are 32-bit elements; how exact they have to be, the bound alone decides.
A program may use at most 64 MiB of HBM per device.

v0:
```python
import jax
import jax.numpy as jnp
from jax import lax
from jax.sharding import PartitionSpec as P

amplitude = 2.0


def from_root(value, axis, source):
    kept = jnp.where(lax.axis_index(axis) == source, value, 0).astype(value.dtype)
    return lax.psum(kept, axis)


def kernel_block(left_side, right_side, weights):
    scaled = left_side * weights[None, :]
    left_square = jnp.sum(scaled * left_side, axis=1)
    right_square = jnp.sum(right_side * right_side * weights[None, :], axis=1)
    cross_term = lax.dot_general(
        scaled,
        right_side,
        (((1,), (1,)), ((), ())),
        precision=lax.Precision.HIGHEST,
        preferred_element_type=jnp.float32,
    )
    return amplitude * jnp.exp(
        -0.5 * (left_square[:, None] + right_square[None, :] - 2.0 * cross_term)
    )


def factor_rows(row_points, chosen, inv_factor, weights):
    kernel_part = kernel_block(row_points, chosen, weights)
    return lax.dot_general(
        kernel_part,
        inv_factor,
        (((1,), (1,)), ((), ())),
        precision=lax.Precision.HIGHEST,
        preferred_element_type=jnp.float32,
    )


def on_device(points, panel_pool, order, panel_index, inv_factor, ard_weights, noise):
    row_count = points.shape[0]
    row_devices = lax.axis_size("row")
    column_devices = lax.axis_size("col")
    col_count = row_count * row_devices // column_devices
    per_group = column_devices // row_devices
    row_place = lax.axis_index("row")
    col_place = lax.axis_index("col")
    owner_row = col_place // per_group
    offset = col_place % per_group * col_count
    own_points = lax.dynamic_slice_in_dim(points, offset, col_count, 0)
    col_points = from_root(own_points, "row", owner_row)
    panel_block = panel_index[0]
    chosen = jnp.take(panel_pool, order, axis=0)
    local_rows = factor_rows(points, chosen, inv_factor, ard_weights)
    rows_panel = from_root(local_rows, "col", panel_block)
    local_part = lax.dynamic_slice_in_dim(rows_panel, offset, col_count, 0)
    cols_panel = from_root(local_part, "row", owner_row)
    kernel_tile = kernel_block(points, col_points, ard_weights)
    row_ids = lax.broadcasted_iota(jnp.int32, (row_count, col_count), 0) + row_place * row_count
    col_ids = lax.broadcasted_iota(jnp.int32, (row_count, col_count), 1) + col_place * col_count
    kernel_tile = kernel_tile + jnp.where(row_ids == col_ids, noise[:, None], jnp.float32(0.0))
    update = lax.dot_general(
        rows_panel,
        cols_panel,
        (((1,), (1,)), ((), ())),
        precision=lax.Precision.HIGHEST,
        preferred_element_type=jnp.float32,
    )
    return kernel_tile - update


def solution(mesh):
    in_specs = (P("row", None), P("col", None), P(), P(), P(), P(), P("row"))
    out_specs = P("row", "col")
    return jax.shard_map(
        on_device, mesh=mesh, in_specs=in_specs, out_specs=out_specs, check_vma=False
    )
```

profile of v0, /device:TPU:2, one launch (start us, length us, event | category | flops | bytes accessed | tf_op | source)
XLA Modules:
  0.0 449.3 jit_solution(17287687813708850016)
XLA Ops:
  6.5 0.0 copy-start
  6.5 0.0 all-reduce.4.cloned.1.call-start
  6.6 1.8 dynamic-slice_select_fusion.1
  8.4 0.0 all-reduce.4.cloned.1.call-update
  8.4 0.0 all-reduce.6.cloned.1.call-start
  8.5 0.7 compare_select_fusion
  9.2 0.7 compare_and_fusion
  10.5 1.3 fusion.17
  11.8 0.0 copy-done.1
  11.8 1.0 gather_fusion
  12.8 3.2 fusion.14
  16.1 133.6 %all-reduce.4.cloned.1.call-done = f32[512,128]{1,0:T(8,128)} async-done(((f32[512,128]{1,0:T(8,128)}), f32[512,128]{1,0:T(8,128)}) %all-reduce.4.cloned.1.call-update) | async-done | bytes 262160 | tf_op jit(solution)/shard_map/psum | solution.py:11
  149.7 1.2 multiply_reduce_fusion.1
  150.9 6.8 %fusion.7 = f32[1024,512]{1,0:T(8,128)} fusion(f32[512,512]{1,0:T(8,128)S(1)} %copy-done, f32[1024,512]{1,0:T(8,128)} %fusion.14, f32[512]{0:T(512)S(1)} %get-tuple-element.6, f32[1024]{0:T(1024)S(1)} %fusion.17, pred[]{:T(512)S(6)} %eq.14), kind=kOutput, calls=%fused_computation.9 | convolution fusion | flops 3224371200 | bytes 5249025 | tf_op jit(solution)/shard_map/dot_general | solution.py:32
  157.7 0.0 all-reduce.6.cloned.1.call-update
  157.7 0.0 all-reduce.8.cloned.1.call-start
  157.8 134.5 %all-reduce.6.cloned.1.call-done = f32[1024,512]{1,0:T(8,128)} async-done(((f32[1024,512]{1,0:T(8,128)}), f32[1024,512]{1,0:T(8,128)}) %all-reduce.6.cloned.1.call-update) | async-done | bytes 2097168 | tf_op jit(solution)/shard_map/psum | solution.py:11
  292.3 2.4 dynamic-slice_select_fusion
  294.8 0.0 all-reduce.8.cloned.1.call-update
  294.8 0.0 copy-start.5
  294.8 0.0 copy-start.7
  294.8 139.4 %all-reduce.8.cloned.1.call-done = f32[512,512]{1,0:T(8,128)} async-done(((f32[512,512]{1,0:T(8,128)}), f32[512,512]{1,0:T(8,128)}) %all-reduce.8.cloned.1.call-update) | async-done | bytes 1048592 | tf_op jit(solution)/shard_map/psum | solution.py:11
  434.2 4.7 %fusion.26 = f32[1024,512]{1,0:T(8,128)S(1)} fusion(f32[1024,512]{1,0:T(8,128)S(1)} %copy-done.2, f32[512,512]{1,0:T(8,128)} %all-reduce.8.cloned.1.call-done), kind=kOutput, calls=%fused_computation.36 | convolution fusion | flops 3221225472 | bytes 5242880 | tf_op jit(solution)/shard_map/dot_general | solution.py:63
  439.0 3.7 add_subtract_fusion
  (15 shorter events, 0.0 us)
Async XLA Ops:
  6.5 144.4 %copy-start = (f32[512,512]{1,0:T(8,128)S(1)}, f32[512,512]{1,0:T(8,128)}, u32[]{:S(2)}) copy-start(f32[512,512]{1,0:T(8,128)} %param.11) | copy-start | bytes 3145732
  6.5 6.3 %copy-start.3 = (f32[1024,128]{1,0:T(8,128)S(1)}, f32[1024,128]{1,0:T(8,128)}, u32[]{:S(2)}) copy-start(f32[1024,128]{1,0:T(8,128)} %param.7) | copy-start | bytes 1572868
  6.5 6.3 %copy-start.6 = (f32[128]{0:T(128)S(1)}, f32[128]{0:T(128)}, u32[]{:S(2)}) copy-start(f32[128]{0:T(128)} %param.12) | copy-start | bytes 1540
  6.5 5.2 %copy-start.1 = (f32[512,128]{1,0:T(8,128)S(1)}, f32[512,128]{1,0:T(8,128)}, u32[]{:S(2)}) copy-start(f32[512,128]{1,0:T(8,128)} %param.8) | copy-start | bytes 786436
  6.5 143.1 %all-reduce.4.cloned.1.call-start = ((), (), s32[]{:S(2)}) async-start(), calls=%async_computation | async-start | bytes 524288 | tf_op jit(solution)/shard_map/psum | solution.py:11
  8.4 283.9 %all-reduce.6.cloned.1.call-start = ((), (), s32[]{:S(2)}) async-start(), calls=%async_computation.1 | async-start | bytes 4194304 | tf_op jit(solution)/shard_map/psum | solution.py:11
  157.7 276.5 %all-reduce.8.cloned.1.call-start = ((), (), s32[]{:S(2)}) async-start(), calls=%async_computation.2 | async-start | bytes 2097152 | tf_op jit(solution)/shard_map/psum | solution.py:11
  292.3 141.9 %copy-start.2 = (f32[1024,512]{1,0:T(8,128)S(1)}, f32[1024,512]{1,0:T(8,128)}, u32[]{:S(2)}) copy-start(f32[1024,512]{1,0:T(8,128)} %all-reduce.6.cloned.1.call-done) | copy-start | bytes 6291460
  294.8 144.2 %copy-start.5 = (f32[512,128]{1,0:T(8,128)S(1)}, f32[512,128]{1,0:T(8,128)}, u32[]{:S(2)}) copy-start(f32[512,128]{1,0:T(8,128)} %all-reduce.4.cloned.1.call-done) | copy-start | bytes 786436
  294.8 144.2 %copy-start.7 = (f32[1024]{0:T(1024)S(1)}, f32[1024]{0:T(1024)}, u32[]{:S(2)}) copy-start(f32[1024]{0:T(1024)} %param.13) | copy-start | bytes 12292
  434.2 4.8 %copy-start.4 = (f32[1024,128]{1,0:T(8,128)S(1)}, f32[1024,128]{1,0:T(8,128)}, u32[]{:S(2)}) copy-start(f32[1024,128]{1,0:T(8,128)} %param.7) | copy-start | bytes 1572868
Sparse Core Ops, SparseCore 0:
  9.7 139.9 all-reduce.3
  157.9 134.4 all-reduce.5
  294.9 139.2 all-reduce.7
where the time goes:
time: 450 us; the launch traced here: 449 us
  waiting for transfers between devices  408 us (91%)
  matrix products  18.5 us (4%)
  between operations  13.9 us (3%)
  other arithmetic  8.11 us (2%)
    psum x3, waiting for transfers between devices, from_root(): return lax.psum(kept, axis)  408 us
  transfers between devices with their start and end apart: 3, of which 3 were waited for; matrix products, arithmetic and copies ran while one was open for 2% of the time, Pallas kernels for 0%

commit v1 on v0

v1 whole, which is shorter than its diff:
```python
import functools

import jax
import jax.numpy as jnp
from jax import lax
from jax.experimental import pallas as pl
from jax.experimental.pallas import tpu as pltpu
from jax.sharding import PartitionSpec as P

MESH = pl.DeviceIdType.MESH
F32, BF16 = jnp.float32, jnp.bfloat16
FEAT = 128
PANEL = 512
ROWS = 1024
COLS = 512
NZ, NY, NX = 16, 4, 4
GROUP = NY * NX * 2
PIECE = PANEL // GROUP
SLICE = COLS // NY
REACH = 5


def dot_nt(a, b):
    return lax.dot_general(a, b, (((1,), (1,)), ((), ())), preferred_element_type=F32)


def dot_nn(a, b):
    return lax.dot_general(a, b, (((1,), (0,)), ((), ())), preferred_element_type=F32)


def split2(x):
    high = x.astype(BF16)
    return high, (x - high.astype(F32)).astype(BF16)


def split3(x):
    high = x.astype(BF16)
    rest = x - high.astype(F32)
    mid = rest.astype(BF16)
    return high, mid, (rest - mid.astype(F32)).astype(BF16)


def place():
    z, col = lax.axis_index("row"), lax.axis_index("col")
    return z, col // 8, col // 2 % 4, col % 2


def wrap(z):
    return lax.rem(z + NZ, NZ)


def gather_kernel(
    index_ref, order_ref, pool_ref, points_ref, col_out, chosen_out,
    mixed, landed, chosen, relay, cols,
    b_send, b_recv, one_send, one_recv, two_send, two_recv, local_sem,
):
    z, y, x, core = place()
    me = lax.axis_index("col")
    role = lax.rem(z - x + NZ, 4)
    home = 4 * y + x
    away = wrap(z - home)
    near = (away <= 2) | (away >= 14)
    holder = jnp.where(near, home, jnp.where(away <= 8, wrap(home + REACH), wrap(home - REACH)))
    group = jnp.where(role == 0, z, jnp.where(role == 1, wrap(z - REACH), wrap(z + REACH)))
    line = group // 4
    mine = line == y

    def column(y_place, core_place):
        return (y_place * 4 + x) * 2 + core_place

    barrier = pltpu.get_barrier_semaphore()

    @pl.when(role == 1)
    def _():
        pl.semaphore_signal(barrier, inc=1, device_id=(wrap(z - REACH), me), device_id_type=MESH)

    @pl.when(role == 3)
    def _():
        pl.semaphore_signal(barrier, inc=1, device_id=(wrap(z + REACH), me), device_id_type=MESH)

    for other in range(NY):
        @pl.when((away != 0) & ~((holder == z) & (other == y)))
        def _(other=other):
            pl.semaphore_signal(barrier, inc=1, device_id=(holder, column(other, core)), device_id_type=MESH)

    def greet(step, carry):
        pl.semaphore_signal(barrier, inc=1, device_id=(z, lax.rem(me + step, GROUP)), device_id_type=MESH)
        return carry

    lax.fori_loop(1, GROUP, greet, 0)

    pick = jnp.where(
        lax.broadcasted_iota(jnp.int32, (PANEL, PANEL), 0) == order_ref[...], 1.0, 0.0
    ).astype(BF16)
    parts = [
        lax.dot_general(pick, part, (((0,), (0,)), ((), ())), preferred_element_type=F32)
        for part in split3(pool_ref[...])
    ]
    mixed[...] = (parts[0] + parts[1]) + parts[2]

    expected = GROUP - 1 + jnp.where(
        role == 0, 6, jnp.where(role == 1, 6 - mine, jnp.where(role == 3, 5 - mine, 0))
    )
    pl.semaphore_wait(barrier, expected)

    own_slice = points_ref.at[pl.ds(pl.multiple_of(core * COLS + y * SLICE, SLICE), SLICE)]
    here = cols.at[pl.ds(pl.multiple_of(y * SLICE, SLICE), SLICE)]

    def leg_one(sign, place_id):
        return pltpu.make_async_remote_copy(
            src_ref=own_slice, dst_ref=relay, send_sem=one_send.at[place_id], recv_sem=one_recv,
            device_id=(wrap(z + sign * REACH), me), device_id_type=MESH,
        )

    def leg_two(source, offset, place_id):
        return pltpu.make_async_remote_copy(
            src_ref=source, dst_ref=here, send_sem=two_send.at[place_id], recv_sem=two_recv.at[y],
            device_id=(wrap(z + offset), column(line, core)), device_id_type=MESH,
        )

    @pl.when(role == 0)
    def _():
        leg_one(1, 0).start()
        leg_one(-1, 1).start()
        for place_id, offset in enumerate((-2, 2, -1, 1)):
            leg_two(own_slice, offset, place_id).start()

    def spread(step, carry):
        other = lax.rem(me + step, GROUP)
        pltpu.make_async_remote_copy(
            src_ref=mixed.at[pl.ds(pl.multiple_of(other * PIECE, PIECE), PIECE)],
            dst_ref=landed.at[me], send_sem=b_send.at[0], recv_sem=b_recv.at[0],
            device_id=(z, other), device_id_type=MESH,
        ).start()
        return carry

    lax.fori_loop(1, GROUP, spread, 0)
    my_rows = pl.ds(pl.multiple_of(me * PIECE, PIECE), PIECE)
    landed[me] = mixed[my_rows]
    whole = landed.at[pl.ds(0, GROUP - 1)]
    pltpu.make_async_copy(whole, whole, b_recv.at[0]).wait()
    chosen[my_rows] = landed[index_ref[0]]

    def share(step, carry):
        other = lax.rem(me + step, GROUP)
        pltpu.make_async_remote_copy(
            src_ref=chosen.at[my_rows], dst_ref=chosen.at[my_rows],
            send_sem=b_send.at[1], recv_sem=b_recv.at[1],
            device_id=(z, other), device_id_type=MESH,
        ).start()
        return carry

    lax.fori_loop(1, GROUP, share, 0)

    @pl.when((role == 1) | (role == 3))
    def _():
        leg_one(1, 0).wait_recv()
        for place_id, offset in enumerate((3, -2, 2, -1, 1, 0)):
            if offset == 3:
                wanted = role == 1
            elif offset == 0:
                wanted = ~mine
            else:
                wanted = None
            if wanted is None:
                leg_two(relay, offset, place_id).start()
            else:
                @pl.when(wanted)
                def _(offset=offset, place_id=place_id):
                    leg_two(relay, offset, place_id).start()

        @pl.when(mine)
        def _():
            pltpu.make_async_copy(relay, here, local_sem).start()
            pltpu.make_async_copy(relay, here, local_sem).wait()

    @pl.when(away == 0)
    def _():
        block = points_ref.at[pl.ds(pl.multiple_of(core * COLS, COLS), COLS)]
        pltpu.make_async_copy(block, cols, local_sem).start()
        pltpu.make_async_copy(block, cols, local_sem).wait()

    some = chosen.at[pl.ds(0, (GROUP - 1) * PIECE)]
    pltpu.make_async_copy(some, some, b_recv.at[1]).wait()
    chosen_out[...] = chosen[...]

    for other in range(NY):
        @pl.when((away != 0) & ~((holder == z) & (other == y)))
        def _(other=other):
            piece = cols.at[pl.ds(other * SLICE, SLICE)]
            pltpu.make_async_copy(piece, piece, two_recv.at[other]).wait()
    col_out[...] = cols[...]

    pltpu.make_async_copy(some, some, b_send.at[0]).wait()
    pltpu.make_async_copy(some, some, b_send.at[1]).wait()

    @pl.when(role == 0)
    def _():
        leg_one(1, 0).wait_send()
        leg_one(-1, 1).wait_send()
        for place_id, offset in enumerate((-2, 2, -1, 1)):
            leg_two(own_slice, offset, place_id).wait_send()

    @pl.when((role == 1) | (role == 3))
    def _():
        for place_id in range(1, 5):
            leg_two(relay, 1, place_id).wait_send()

        @pl.when(role == 1)
        def _():
            leg_two(relay, 3, 0).wait_send()

        @pl.when(~mine)
        def _():
            leg_two(relay, 0, 5).wait_send()


def gather_points(index, order, pool, points):
    shape = jax.ShapeDtypeStruct((PANEL, FEAT), F32)
    vmem = pl.BlockSpec(memory_space=pltpu.VMEM)
    return pl.pallas_call(
        gather_kernel,
        out_shape=(shape, shape),
        in_specs=[pl.BlockSpec(memory_space=pltpu.SMEM), vmem, vmem, pl.BlockSpec(memory_space=pl.ANY)],
        out_specs=(vmem, vmem),
        scratch_shapes=[
            pltpu.VMEM((PANEL, FEAT), F32),
            pltpu.VMEM((GROUP, PIECE, FEAT), F32),
            pltpu.VMEM((PANEL, FEAT), F32),
            pltpu.VMEM((SLICE, FEAT), F32),
            pltpu.VMEM((COLS, FEAT), F32),
            pltpu.SemaphoreType.DMA((2,)),
            pltpu.SemaphoreType.DMA((2,)),
            pltpu.SemaphoreType.DMA((2,)),
            pltpu.SemaphoreType.DMA,
            pltpu.SemaphoreType.DMA((6,)),
            pltpu.SemaphoreType.DMA((NY,)),
            pltpu.SemaphoreType.DMA,
        ],
        compiler_params=pltpu.CompilerParams(
            collective_id=0, has_side_effects=True, vmem_limit_bytes=24 * 2**20
        ),
        cost_estimate=pl.CostEstimate(flops=2 * 3 * PANEL * PANEL * FEAT, bytes_accessed=2**21, transcendentals=0),
        name="gather_points",
    )(index, order, pool, points)


def row_norms(scaled):
    return -0.5 * jnp.sum(scaled * scaled, axis=1, keepdims=True)


def column_norms(scaled):
    ones = jnp.ones((8, FEAT), F32)
    total = lax.dot_general(
        ones, scaled * scaled, (((1,), (1,)), ((), ())),
        precision=lax.Precision.HIGHEST, preferred_element_type=F32,
    )
    return -0.5 * total[0:1]


def sides(points, root):
    high, low = split2(points * root)
    kept = high.astype(F32) + low.astype(F32)
    return high, low, kept


def kern(left, right):
    left_high, left_low, left_norm = left
    right_high, right_low, right_norm = right
    pair = jnp.concatenate([left_high, left_low], axis=1)
    cross = dot_nt(pair, jnp.concatenate([right_high, right_high], axis=1))
    cross += dot_nt(pair, jnp.concatenate([right_low, right_low], axis=1))
    return 2.0 * jnp.exp(cross + left_norm + right_norm)


def triple_nt(a, b):
    return dot_nt(a[0], b[0]) + (dot_nt(a[0], b[1]) + dot_nt(a[1], b[0]))


def triple_nn(a, b):
    return dot_nn(a[0], b[0]) + (dot_nn(a[0], b[1]) + dot_nn(a[1], b[0]))


def tile_kernel(
    block, points_ref, col_ref, chosen_ref, inv_ref, weight_ref, noise_ref, out_ref,
    ch_high, ch_low, ch_norm, co_high, co_low, co_norm, h_high, h_low,
):
    z, col = lax.axis_index("row"), lax.axis_index("col")
    step = pl.program_id(0)
    root = jnp.sqrt(weight_ref[...])
    half = PANEL // 2

    @pl.when(step == 0)
    def _():
        high, low, kept = sides(chosen_ref[...], root)
        ch_high[...], ch_low[...], ch_norm[...] = high, low, column_norms(kept)
        high_c, low_c, kept_c = sides(col_ref[...], root)
        co_high[...], co_low[...], co_norm[...] = high_c, low_c, column_norms(kept_c)
        side = kern((high_c, low_c, row_norms(kept_c)), (high, low, ch_norm[...]))
        k_high, k_low = split2(side)
        inv = split2(inv_ref[...])
        first = triple_nt([k_high[:, :half], k_low[:, :half]], [w[:half, :half] for w in inv])
        second = triple_nt([k_high, k_low], [w[half:, :] for w in inv])
        first, second = split2(first), split2(second)
        both = [jnp.concatenate([a, b], axis=1) for a, b in zip(first, second)]
        left = triple_nn(both, [w[:, :half] for w in inv])
        right = triple_nn(second, [w[half:, half:] for w in inv])
        h_high[:, :half], h_low[:, :half] = split2(left)
        h_high[:, half:], h_low[:, half:] = split2(right)

    high, low, kept = sides(points_ref[...], root)
    norm = row_norms(kept)
    panel = split2(kern((high, low, norm), (ch_high[...], ch_low[...], ch_norm[...])))
    update = triple_nt(panel, (h_high[...], h_low[...]))
    tile = kern((high, low, norm), (co_high[...], co_low[...], co_norm[...]))
    row_ids = lax.broadcasted_iota(jnp.int32, (block, COLS), 0) + step * block + z * ROWS
    col_ids = lax.broadcasted_iota(jnp.int32, (block, COLS), 1) + col * COLS
    first_noise = pl.multiple_of(col % 2 * COLS, COLS)
    noise = noise_ref[:, pl.ds(first_noise, COLS)]
    out_ref[...] = tile + jnp.where(row_ids == col_ids, noise, 0.0) - update


def make_tile(points, cols, chosen, inv_factor, weights, noise):
    block = 256
    full = lambda shape: pl.BlockSpec(shape, lambda i: (0, 0))
    return pl.pallas_call(
        functools.partial(tile_kernel, block),
        grid=(ROWS // block,),
        out_shape=jax.ShapeDtypeStruct((ROWS, COLS), F32),
        in_specs=[
            pl.BlockSpec((block, FEAT), lambda i: (i, 0)),
            full((COLS, FEAT)), full((PANEL, FEAT)), full((PANEL, PANEL)), full((1, FEAT)), full((1, ROWS)),
        ],
        out_specs=pl.BlockSpec((block, COLS), lambda i: (i, 0)),
        scratch_shapes=[
            pltpu.VMEM((PANEL, FEAT), BF16), pltpu.VMEM((PANEL, FEAT), BF16), pltpu.VMEM((1, PANEL), F32),
            pltpu.VMEM((COLS, FEAT), BF16), pltpu.VMEM((COLS, FEAT), BF16), pltpu.VMEM((1, COLS), F32),
            pltpu.VMEM((COLS, PANEL), BF16), pltpu.VMEM((COLS, PANEL), BF16),
        ],
        compiler_params=pltpu.CompilerParams(vmem_limit_bytes=32 * 2**20),
        cost_estimate=pl.CostEstimate(flops=4 * 10**9, bytes_accessed=5 * 2**20, transcendentals=2**20),
        name="make_tile",
    )(points, cols, chosen, inv_factor, weights, noise)


def on_device(points, panel_pool, order, panel_index, inv_factor, ard_weights, noise):
    cols, chosen = gather_points(panel_index, order.reshape(1, PANEL), panel_pool, points)
    return make_tile(points, cols, chosen, inv_factor, ard_weights.reshape(1, FEAT), noise.reshape(1, ROWS))


def solution(mesh):
    in_specs = (P("row", None), P("col", None), P(), P(), P(), P(), P("row"))
    return jax.shard_map(
        on_device, mesh=mesh, in_specs=in_specs, out_specs=P("row", "col"), check_vma=False
    )
```

time: 450 us -> 43.9 us (0.10)
  the two profiles are of different devices: /device:TPU:2 before, /device:TPU:6 now
where the time goes in v1:
time: 43.9 us; the launch traced here: 43.6 us
  Pallas kernels  36.6 us (83%)
  local copies, waits for them, and re-layouts  6.27 us (14%)
  between operations  0.68 us (2%)
    pallas_call x1, Pallas kernels, gather_points(): pl.pallas_call(gather_kernel, out_shape=(shape, shape), in_specs=[pl.Bloc...  28.6 us
    pallas_call x1, Pallas kernels, make_tile(): pl.pallas_call(functools.partial(tile_kernel, block), grid=(ROWS // block...  8.06 us
    unnamed x14, local copies, waits for them, and re-layouts  6.27 us

profile of v1, /device:TPU:6, one launch (start us, length us, event | category | flops | bytes accessed | tf_op | source)
XLA Modules:
  0.0 43.6 jit_solution(10024506849805431496)
XLA Ops:
  0.7 0.0 copy-start
  0.7 1.0 %copy-done = f32[1024,128]{1,0:T(8,128)S(1)} copy-done((f32[1024,128]{1,0:T(8,128)S(1)}, f32[1024,128]{1,0:T(8,128)}, u32[]{:S(2)}) %copy-start) | copy-done | bytes 524312
  1.7 0.0 copy-start.2
  1.7 0.9 %copy-done.2 = f32[512,128]{1,0:T(8,128)S(1)} copy-done((f32[512,128]{1,0:T(8,128)S(1)}, f32[512,128]{1,0:T(8,128)}, u32[]{:S(2)}) %copy-start.2) | copy-done | bytes 262168
  2.6 0.0 copy-start.3
  2.6 0.7 %copy-done.3 = s32[512]{0:T(512)S(1)} copy-done((s32[512]{0:T(512)S(1)}, s32[512]{0:T(512)}, u32[]{:S(2)}) %copy-start.3) | copy-done | bytes 2072
  3.3 28.6 %gather_points.1 = (f32[512,128]{1,0:T(8,128)S(1)}, f32[512,128]{1,0:T(8,128)S(1)}) custom-call(s32[1]{0:T(128)S(6)} %copy.8.index_ref, s32[1,512]{1,0:T(1,128)S(1)} %bitcast.3, f32[512,128]{1,0:T(8,128)S(1)} %copy-done.2, f32[1024,128]{1,0:T(8,128)S(1)} %copy-done), custom_call_target="tpu_custom_call" | custom-call | flops 201326592 | bytes 2097152 | tf_op jit(solution)/shard_map/gather_points/pallas_call | solution.py:221
  31.9 0.0 copy-start.1
  31.9 1.0 %copy-done.1 = f32[1024,128]{1,0:T(8,128)S(1)} copy-done((f32[1024,128]{1,0:T(8,128)S(1)}, f32[1024,128]{1,0:T(8,128)}, u32[]{:S(2)}) %copy-start.1) | copy-done | bytes 524312
  33.0 0.0 copy-start.4
  33.0 1.2 %copy-done.4 = f32[512,512]{1,0:T(8,128)S(1)} copy-done((f32[512,512]{1,0:T(8,128)S(1)}, f32[512,512]{1,0:T(8,128)}, u32[]{:S(2)}) %copy-start.4) | copy-done | bytes 1048600
  34.2 0.0 copy-start.5
  34.2 0.7 %copy-done.5 = f32[1024]{0:T(1024)S(1)} copy-done((f32[1024]{0:T(1024)S(1)}, f32[1024]{0:T(1024)}, u32[]{:S(2)}) %copy-start.5) | copy-done | bytes 4120
  34.9 0.0 copy-start.6
  34.9 0.7 %copy-done.6 = f32[128]{0:T(128)S(1)} copy-done((f32[128]{0:T(128)S(1)}, f32[128]{0:T(128)}, u32[]{:S(2)}) %copy-start.6) | copy-done | bytes 536
  35.5 8.1 %make_tile.1 = f32[1024,512]{1,0:T(8,128)} custom-call(f32[1024,128]{1,0:T(8,128)S(1)} %copy-done.1, f32[512,128]{1,0:T(8,128)S(1)} %get-tuple-element.7.col_ref, f32[512,128]{1,0:T(8,128)S(1)} %get-tuple-element.8.chosen_ref, f32[512,512]{1,0:T(8,128)S(1)} %copy-done.4, f32[1,128]{1,0:T(1,128)S(1)} %bitcast.5, f32[1,1024]{1,0:T(1,128)S(1)} %bitcast.4), custom_call_target="tpu_custom_call" | custom-call | flops 4000000000 | bytes 5242880 | tf_op jit(solution)/shard_map/make_tile/pallas_call | solution.py:326
Async XLA Ops:
  0.7 1.0 %copy-start = (f32[1024,128]{1,0:T(8,128)S(1)}, f32[1024,128]{1,0:T(8,128)}, u32[]{:S(2)}) copy-start(f32[1024,128]{1,0:T(8,128)} %points_ref.3) | copy-start | bytes 1572868
  1.7 0.9 %copy-start.2 = (f32[512,128]{1,0:T(8,128)S(1)}, f32[512,128]{1,0:T(8,128)}, u32[]{:S(2)}) copy-start(f32[512,128]{1,0:T(8,128)} %pool_ref.1) | copy-start | bytes 786436
  2.6 0.7 %copy-start.3 = (s32[512]{0:T(512)S(1)}, s32[512]{0:T(512)}, u32[]{:S(2)}) copy-start(s32[512]{0:T(512)} %param.9) | copy-start | bytes 6148
  31.9 1.0 %copy-start.1 = (f32[1024,128]{1,0:T(8,128)S(1)}, f32[1024,128]{1,0:T(8,128)}, u32[]{:S(2)}) copy-start(f32[1024,128]{1,0:T(8,128)} %points_ref.3) | copy-start | bytes 1572868
  33.0 1.2 %copy-start.4 = (f32[512,512]{1,0:T(8,128)S(1)}, f32[512,512]{1,0:T(8,128)}, u32[]{:S(2)}) copy-start(f32[512,512]{1,0:T(8,128)} %inv_ref.1) | copy-start | bytes 3145732
  34.2 0.7 %copy-start.5 = (f32[1024]{0:T(1024)S(1)}, f32[1024]{0:T(1024)}, u32[]{:S(2)}) copy-start(f32[1024]{0:T(1024)} %param.13) | copy-start | bytes 12292
  34.9 0.7 %copy-start.6 = (f32[128]{0:T(128)S(1)}, f32[128]{0:T(128)}, u32[]{:S(2)}) copy-start(f32[128]{0:T(128)} %param.12) | copy-start | bytes 1540

commit v2 on v0

v2 whole, which is shorter than its diff:
```python
import functools

import jax
import jax.numpy as jnp
from jax import lax
from jax.experimental import pallas as pl
from jax.experimental.pallas import tpu as pltpu
from jax.sharding import PartitionSpec as P

MESH = pl.DeviceIdType.MESH
F32, BF16 = jnp.float32, jnp.bfloat16
FEAT = 128
PANEL = 512
ROWS = 1024
COLS = 512
NZ, NY, NX = 16, 4, 4
SLICE = COLS // NY
TEAM = NY * 2
GROUP = NX * TEAM
PIECE = PANEL // GROUP
REACH = 5
SAME = 15
BLOCK = 256


def dot_nt(a, b):
    return lax.dot_general(a, b, (((1,), (1,)), ((), ())), preferred_element_type=F32)


def triple_nt(a, b):
    return dot_nt(a[0], b[0]) + (dot_nt(a[0], b[1]) + dot_nt(a[1], b[0]))


def dot_nn(a, b):
    return lax.dot_general(a, b, (((1,), (0,)), ((), ())), preferred_element_type=F32)


def triple_nn(a, b):
    return dot_nn(a[0], b[0]) + (dot_nn(a[0], b[1]) + dot_nn(a[1], b[0]))


def split2(x):
    high = x.astype(BF16)
    return high, (x - high.astype(F32)).astype(BF16)


def scaled_pair(points, root):
    high, low = split2(points * root)
    return jnp.concatenate([high, low], axis=1), high.astype(F32) + low.astype(F32)


def row_norms(kept):
    return -0.5 * jnp.sum(kept * kept, axis=1, keepdims=True)


def column_norms(kept):
    total = lax.dot_general(
        jnp.ones((8, FEAT), F32), kept * kept, (((1,), (1,)), ((), ())),
        precision=lax.Precision.HIGHEST, preferred_element_type=F32,
    )
    return -0.5 * total[0:1]


def kern(left, left_norm, right, right_norm):
    high, low = right[:, :FEAT], right[:, FEAT:]
    cross = dot_nt(left, jnp.concatenate([high, high], axis=1))
    cross += dot_nt(left, jnp.concatenate([low, low], axis=1))
    return 2.0 * jnp.exp(cross + left_norm + right_norm)


def column(y, x, core):
    return (y * NX + x) * 2 + core


def wrap(z):
    return lax.rem(z + NZ, NZ)


def gather_kernel(
    index_ref, order_ref, pool_ref, points_ref, inv_ref, weight_ref, noise_ref,
    col_out, pan_out, pan_norm, pair_out, norm_out, g_high, g_low, root_out, noise_out,
    order_v, points_v, inv_v, weight_v, w_high, w_low, landed, chosen, relay, cols,
    load_sem, ready_near, ready_plane, ready_plus, ready_minus, ready_two,
    one_send, one_recv, two_send, two_recv, b_send, b_recv,
):
    z, me = lax.axis_index("row"), lax.axis_index("col")
    y, x, core = me // 8, me // 2 % 4, me % 2
    seat = y * 2 + core
    home = NX * y + x
    role = wrap(z - x) % 4
    is_source = role == 0
    is_relay = (role == 1) | (role == 3)
    group = jnp.where(is_source, z, jnp.where(role == 1, wrap(z - REACH), wrap(z + REACH)))
    line = group // 4
    plus, minus = wrap(z + REACH), wrap(z - REACH)

    def skips(relay_place, target_place):
        return (relay_place >= NZ // 2) & (target_place < 4)

    away = wrap(z - home)
    middle = jnp.where(away <= 8, wrap(home + REACH), wrap(home - REACH))
    near = (away <= 2) | (away >= 14) | skips(middle, z)
    holder = jnp.where(near, home, middle)
    served = (away != 0) & (holder != z)

    def signal(sem, device):
        pl.semaphore_signal(sem, inc=1, device_id=device, device_id_type=MESH)

    def wait_for(sem, amount):
        @pl.when(amount > 0)
        def _():
            pl.semaphore_wait(sem, amount)

    def each(low, high, do):
        def body(i, carry):
            do(i)
            return carry
        lax.fori_loop(low, high, body, 0)

    def others(low, high, but, do):
        each(low, but, do)
        each(but + 1, high, do)

    def team(other):
        return (z, column(other // 2, x, other % 2))

    def across(other):
        return (z, column(y, other, core))

    def holders(other):
        return (holder, column(other, x, core))

    def target(place):
        return (place, column(line, x, core))

    own = [(is_source, wrap(z + o)) for o in (-2, 2, -1, 1)]
    skipped = []
    for d in range(3, 14):
        through = plus if d <= 8 else minus
        skipped.append((is_source & skips(through, wrap(z + d)), wrap(z + d)))
    passed = [
        ((role == 1 if o == 3 else is_relay) & ~skips(z, wrap(z + o)), wrap(z + o))
        for o in (3, -2, 2, -1, 1)
    ]
    first = own + skipped
    legs = [(is_source, plus), (is_source, minus)]
    sent = jnp.where(role == 1, minus, plus)

    def count(pairs, test):
        return sum(jnp.where(applies & test(place), 1, 0) for applies, place in pairs)

    lower = lambda place: place < z
    higher = lambda place: place > z

    barrier = pltpu.get_barrier_semaphore()

    @pl.when(served & (holder > z))
    def _():
        each(0, NY, lambda i: signal(barrier, holders(i)))

    @pl.when(is_relay & (sent > z))
    def _():
        signal(barrier, (sent, me))

    for applies, place in first + passed:
        @pl.when(applies & (place > z))
        def _(place=place):
            signal(barrier, target(place))

    for applies, place in legs:
        @pl.when(applies & (place > z))
        def _(place=place):
            signal(barrier, (place, me))

    each(seat + 1, TEAM, lambda i: signal(barrier, team(i)))
    each(x + 1, NX, lambda i: signal(barrier, across(i)))

    loads = [
        pltpu.make_async_copy(a, b, load_sem.at[i])
        for i, (a, b) in enumerate((
            (inv_ref, inv_v), (order_ref, order_v), (weight_ref, weight_v), (points_ref, points_v), (noise_ref, noise_out),
        ))
    ]
    for load in loads:
        load.start()

    expected = (
        seat + x + count(first + passed + legs, lower)
        + jnp.where(served & (holder < z), NY, 0) + jnp.where(is_relay & (sent < z), 1, 0)
    )
    wait_for(barrier, expected)

    own_slice = points_ref.at[pl.ds(pl.multiple_of(core * COLS + y * SLICE, SLICE), SLICE)]
    here = cols.at[pl.ds(pl.multiple_of(y * SLICE, SLICE), SLICE)]

    def leg_one(place, number):
        return pltpu.make_async_remote_copy(
            src_ref=own_slice, dst_ref=relay, send_sem=one_send.at[number], recv_sem=one_recv,
            device_id=(place, me), device_id_type=MESH,
        )

    def leg_two(from_ref, place, number):
        return pltpu.make_async_remote_copy(
            src_ref=from_ref, dst_ref=here, send_sem=two_send.at[number], recv_sem=two_recv.at[y],
            device_id=target(place), device_id_type=MESH,
        )

    def start_one(test):
        for number, (applies, place) in enumerate(legs):
            @pl.when(applies & test(number, place))
            def _(number=number, place=place):
                leg_one(place, number).start()

    def start_two(pairs, from_ref, test):
        for number, (applies, place) in enumerate(pairs):
            @pl.when(applies & test(place))
            def _(number=number, place=place):
                leg_two(from_ref, place, number).start()

    start_one(lambda number, place: place < z)
    start_two(first, own_slice, lower)

    each(0, seat, lambda i: signal(ready_near, team(i)))
    each(0, x, lambda i: signal(ready_near, across(i)))

    @pl.when(is_relay & (sent < z) & (role == 1))
    def _():
        signal(ready_plus, (sent, me))

    @pl.when(is_relay & (sent < z) & (role == 3))
    def _():
        signal(ready_minus, (sent, me))

    @pl.when(served & (holder < z))
    def _():
        each(0, NY, lambda i: signal(ready_two, holders(i)))

    wait_for(ready_near, (TEAM - 1 - seat) + (NX - 1 - x))
    others(0, NX, x, lambda i: signal(ready_plane, across(i)))
    pl.semaphore_wait(ready_plane, NX - 1)

    my_rows = pl.ds(pl.multiple_of(me * PIECE, PIECE), PIECE)

    def spread(step):
        other = lax.rem(me + step, GROUP)
        pltpu.make_async_remote_copy(
            src_ref=pool_ref.at[pl.ds(pl.multiple_of(other * PIECE, PIECE), PIECE)], dst_ref=landed.at[me],
            send_sem=b_send.at[0], recv_sem=b_recv.at[0], device_id=(z, other), device_id_type=MESH,
        ).start()

    def share(step):
        other = lax.rem(me + step, GROUP)
        pltpu.make_async_remote_copy(
            src_ref=chosen.at[my_rows], dst_ref=chosen.at[my_rows],
            send_sem=b_send.at[1], recv_sem=b_recv.at[1], device_id=(z, other), device_id_type=MESH,
        ).start()

    def wait_bytes(ref, sem):
        pltpu.make_async_copy(ref, ref, sem).wait()

    some = chosen.at[pl.ds(0, (GROUP - 1) * PIECE)]
    each(1, GROUP, spread)
    keep = pltpu.make_async_copy(pool_ref.at[my_rows], landed.at[me], load_sem.at[5])
    keep.start()

    loads[0].wait()
    loads[1].wait()
    pick = jnp.where(
        lax.broadcasted_iota(jnp.int32, (PANEL, PANEL), 0) == order_v[...], 1.0, 0.0
    ).astype(BF16)
    inv_high, inv_low = split2(inv_v[...])
    w_high[...] = dot_nt(inv_high, pick).astype(BF16)
    w_low[...] = dot_nt(inv_low, pick).astype(BF16)

    @pl.when(is_source & (plus > z))
    def _():
        pl.semaphore_wait(ready_plus, 1)
    start_one(lambda number, place: (place > z) & (number == 0))

    wait_bytes(some, b_recv.at[0])
    keep.wait()
    chosen[my_rows] = landed[index_ref[0]]
    each(1, GROUP, share)

    def pass_on():
        @pl.when(is_source & (minus > z))
        def _():
            pl.semaphore_wait(ready_minus, 1)
        start_one(lambda number, place: (place > z) & (number == 1))

        @pl.when(is_relay)
        def _():
            leg_one(plus, 0).wait_recv()
            start_two(passed, relay, lower)

            @pl.when(line != y)
            def _():
                leg_two(relay, z, SAME).start()

            @pl.when(line == y)
            def _():
                copy = pltpu.make_async_copy(relay, here, load_sem.at[0])
                copy.start()
                copy.wait()

        wait_for(ready_two, count(first + passed, higher))
        start_two(first, own_slice, higher)
        start_two(passed, relay, higher)

    @pl.when(z >= NZ // 2)
    def _():
        pass_on()

    loads[2].wait()
    loads[3].wait()
    root = jnp.sqrt(weight_v[...])
    root_out[...] = root
    pair, kept = scaled_pair(points_v[...], root)
    pair_out[...] = pair
    norm_out[...] = jnp.broadcast_to(row_norms(kept), (ROWS, FEAT))

    @pl.when(away == 0)
    def _():
        block = points_ref.at[pl.ds(pl.multiple_of(core * COLS, COLS), COLS)]
        copy = pltpu.make_async_copy(block, cols, load_sem.at[0])
        copy.start()
        copy.wait()

    wait_bytes(some, b_recv.at[1])

    @pl.when(z < NZ // 2)
    def _():
        pass_on()

    pan_pair, pan_kept = scaled_pair(chosen[...], root)
    pan_out[...] = pan_pair
    pan_norm[...] = column_norms(pan_kept)

    @pl.loop(0, ROWS // BLOCK)
    def _(step):
        rows = pl.ds(pl.multiple_of(step * BLOCK, BLOCK), BLOCK)
        part = split2(kern(pair_out[rows], norm_out[rows, 0:1], pan_out[...], pan_norm[...]))
        part = split2(triple_nt(part, (w_high[...], w_low[...])))
        g_high[rows], g_low[rows] = split2(triple_nn(part, (w_high[...], w_low[...])))

    for other in range(NY):
        @pl.when((away != 0) & ~((holder == z) & (other == y)))
        def _(other=other):
            wait_bytes(cols.at[pl.ds(other * SLICE, SLICE)], two_recv.at[other])

    col_out[...] = cols[...]

    wait_bytes(some, b_send.at[0])
    wait_bytes(some, b_send.at[1])
    for number, (applies, place) in enumerate(legs):
        @pl.when(applies)
        def _(number=number, place=place):
            leg_one(place, number).wait_send()
    for pairs, from_ref in ((first, own_slice), (passed, relay)):
        for number, (applies, place) in enumerate(pairs):
            @pl.when(applies)
            def _(number=number, place=place, from_ref=from_ref):
                leg_two(from_ref, place, number).wait_send()

    @pl.when(is_relay & (line != y))
    def _():
        leg_two(relay, z, SAME).wait_send()

    loads[4].wait()


def gather_points(index, order, pool, points, inv_factor, weights, noise):
    vmem = pl.BlockSpec(memory_space=pltpu.VMEM)
    hbm = pl.BlockSpec(memory_space=pltpu.HBM)
    shape = jax.ShapeDtypeStruct
    outs = (
        shape((COLS, FEAT), F32), shape((PANEL, 2 * FEAT), BF16), shape((1, PANEL), F32),
        shape((ROWS, 2 * FEAT), BF16), shape((ROWS, FEAT), F32),
        shape((ROWS, PANEL), BF16), shape((ROWS, PANEL), BF16), shape((1, FEAT), F32), shape((1, ROWS), F32),
    )
    dma, flag = pltpu.SemaphoreType.DMA, pltpu.SemaphoreType.REGULAR
    return pl.pallas_call(
        gather_kernel,
        out_shape=outs,
        in_specs=[pl.BlockSpec(memory_space=pltpu.SMEM)] + [hbm] * 6,
        out_specs=(vmem,) * len(outs),
        scratch_shapes=[
            pltpu.VMEM((1, PANEL), jnp.int32),
            pltpu.VMEM((ROWS, FEAT), F32),
            pltpu.VMEM((PANEL, PANEL), F32),
            pltpu.VMEM((1, FEAT), F32),
            pltpu.VMEM((PANEL, PANEL), BF16),
            pltpu.VMEM((PANEL, PANEL), BF16),
            pltpu.VMEM((GROUP, PIECE, FEAT), F32),
            pltpu.VMEM((PANEL, FEAT), F32),
            pltpu.VMEM((SLICE, FEAT), F32),
            pltpu.VMEM((COLS, FEAT), F32),
            dma((6,)),
            flag, flag, flag, flag, flag,
            dma((2,)),
            dma,
            dma((16,)),
            dma((NY,)),
            dma((2,)),
            dma((2,)),
        ],
        compiler_params=pltpu.CompilerParams(
            collective_id=0, has_side_effects=True, vmem_limit_bytes=40 * 2**20
        ),
        cost_estimate=pl.CostEstimate(flops=5 * 10**9, bytes_accessed=2**22, transcendentals=2**19),
        name="gather_points",
    )(index, order, pool, points, inv_factor, weights, noise)


def tile_kernel(
    col_ref, pan_ref, pan_norm, pair_ref, norm_ref, g_high, g_low, root_ref, noise_ref, out_ref, tile, out_sem,
):
    z, col = lax.axis_index("row"), lax.axis_index("col")
    pair, kept = scaled_pair(col_ref[...], root_ref[...])
    norms = column_norms(kept)
    side = split2(kern(pair, row_norms(kept), pan_ref[...], pan_norm[...]))
    noise = noise_ref[:, pl.ds(pl.multiple_of(col % 2 * COLS, COLS), COLS)]
    copies = []
    for step in range(ROWS // BLOCK):
        rows = pl.ds(step * BLOCK, BLOCK)
        update = triple_nt((g_high[rows], g_low[rows]), side)
        part = kern(pair_ref[rows], norm_ref[rows, 0:1], pair, norms)
        row_ids = lax.broadcasted_iota(jnp.int32, (BLOCK, COLS), 0) + (step * BLOCK + z * ROWS)
        col_ids = lax.broadcasted_iota(jnp.int32, (BLOCK, COLS), 1) + col * COLS
        tile[rows] = part + jnp.where(row_ids == col_ids, noise, 0.0) - update
        copy = pltpu.make_async_copy(tile.at[rows], out_ref.at[rows], out_sem.at[step])
        copy.start()
        copies.append(copy)
    for copy in copies:
        copy.wait()


def make_tile(parts):
    vmem = pl.BlockSpec(memory_space=pltpu.VMEM)
    return pl.pallas_call(
        tile_kernel,
        out_shape=jax.ShapeDtypeStruct((ROWS, COLS), F32),
        in_specs=[vmem] * len(parts),
        out_specs=pl.BlockSpec(memory_space=pltpu.HBM),
        scratch_shapes=[
            pltpu.VMEM((ROWS, COLS), F32),
            pltpu.SemaphoreType.DMA((ROWS // BLOCK,)),
        ],
        compiler_params=pltpu.CompilerParams(vmem_limit_bytes=40 * 2**20),
        cost_estimate=pl.CostEstimate(flops=3 * 10**9, bytes_accessed=2**22, transcendentals=2**19),
        name="make_tile",
    )(*parts)


def on_device(points, panel_pool, order, panel_index, inv_factor, ard_weights, noise):
    keep = lambda value: pltpu.with_memory_space_constraint(value, pltpu.HBM)
    return make_tile(gather_points(
        panel_index, keep(order.reshape(1, PANEL)), keep(panel_pool), keep(points), keep(inv_factor),
        keep(ard_weights.reshape(1, FEAT)), keep(noise.reshape(1, ROWS)),
    ))


def solution(mesh):
    in_specs = (P("row", None), P("col", None), P(), P(), P(), P(), P("row"))
    return jax.shard_map(
        on_device, mesh=mesh, in_specs=in_specs, out_specs=P("row", "col"), check_vma=False
    )
```

time: 450 us -> 37 us (0.08)
  the two profiles are of different devices: /device:TPU:2 before, /device:TPU:1 now
where the time goes in v2:
time: 37 us; the launch traced here: 36.7 us
  Pallas kernels  36 us (97%)
  between operations  0.66 us (2%)
    pallas_call x1, Pallas kernels, gather_points(): pl.pallas_call(gather_kernel, out_shape=outs, in_specs=[pl.BlockSpec(memo...  31.9 us
    pallas_call x1, Pallas kernels, make_tile(): pl.pallas_call(tile_kernel, out_shape=jax.ShapeDtypeStruct((ROWS, COLS),...  4.13 us

profile of v2, /device:TPU:1, one launch (start us, length us, event | category | flops | bytes accessed | tf_op | source)
XLA Modules:
  0.0 36.7 jit_solution(15706864987769116790)
XLA Ops:
  0.7 31.9 %gather_points.1 = (f32[512,128]{1,0:T(8,128)S(1)}, bf16[512,256]{1,0:T(8,128)(2,1)S(1)}, f32[1,512]{1,0:T(1,128)S(1)}, bf16[1024,256]{1,0:T(8,128)(2,1)S(1)}, f...) custom-call(s32[1]{0:T(128)S(6)} %copy.8.index_ref, ...), custom_call_target="tpu_custom_call" | custom-call | flops 5000000000 | bytes 4194304 | tf_op jit(solution)/shard_map/gather_points/pallas_call | solution.py:382
  32.6 4.1 %make_tile.1 = f32[1024,512]{1,0:T(8,128)} custom-call(f32[512,128]{1,0:T(8,128)S(1)} %get-tuple-element.14.col_ref, bf16[512,256]{1,0:T(8,128)(2,1)S(1)} %get-tuple-element.15.pan_ref, f32[1,512]{1,0:T(1,128)S(1)} %get-tuple-element.16.pan_norm, bf16[1024,256]{1,0:T(8,128)(2,1)S(1)} %get-tuple-element.17.pair_ref, ...), custom_call_target="tpu_custom_call" | custom-call | flops 3000000000 | bytes 4194304 | tf_op jit(solution)/shard_map/make_tile/pallas_call | solution.py:440

commit v3 on v2

--- a/solution.py
+++ b/solution.py
@@ -15,12 +15,13 @@
 COLS = 512
 NZ, NY, NX = 16, 4, 4
 SLICE = COLS // NY
-TEAM = NY * 2
-GROUP = NX * TEAM
+GROUP = NX * NY * 2
 PIECE = PANEL // GROUP
 REACH = 5
 SAME = 15
-BLOCK = 256
+HALF = PANEL // 2
+BLOCK = 512
+TILE = 256
 
 
 def dot_nt(a, b):
@@ -42,6 +43,13 @@
 def split2(x):
     high = x.astype(BF16)
     return high, (x - high.astype(F32)).astype(BF16)
+
+
+def split3(x):
+    high = x.astype(BF16)
+    rest = x - high.astype(F32)
+    mid = rest.astype(BF16)
+    return high, mid, (rest - mid.astype(F32)).astype(BF16)
 
 
 def scaled_pair(points, root):
@@ -79,13 +87,12 @@
 def gather_kernel(
     index_ref, order_ref, pool_ref, points_ref, inv_ref, weight_ref, noise_ref,
     col_out, pan_out, pan_norm, pair_out, norm_out, g_high, g_low, root_out, noise_out,
-    order_v, points_v, inv_v, weight_v, w_high, w_low, landed, chosen, relay, cols,
-    load_sem, ready_near, ready_plane, ready_plus, ready_minus, ready_two,
+    order_v, points_v, inv_v, weight_v, pool_v, mixed, w_high, w_low, landed, chosen, relay, cols,
+    load_sem, ready_plus, ready_minus, ready_two,
     one_send, one_recv, two_send, two_recv, b_send, b_recv,
 ):
     z, me = lax.axis_index("row"), lax.axis_index("col")
     y, x, core = me // 8, me // 2 % 4, me % 2
-    seat = y * 2 + core
     home = NX * y + x
     role = wrap(z - x) % 4
     is_source = role == 0
@@ -99,7 +106,7 @@
 
     away = wrap(z - home)
     middle = jnp.where(away <= 8, wrap(home + REACH), wrap(home - REACH))
-    near = (away <= 2) | (away >= 14) | skips(middle, z)
+    near = (away <= 2) | (away >= 14) | ((away > 8) & skips(middle, z))
     holder = jnp.where(near, home, middle)
     served = (away != 0) & (holder != z)
 
@@ -121,12 +128,6 @@
         each(low, but, do)
         each(but + 1, high, do)
 
-    def team(other):
-        return (z, column(other // 2, x, other % 2))
-
-    def across(other):
-        return (z, column(y, other, core))
-
     def holders(other):
         return (holder, column(other, x, core))
 
@@ -135,11 +136,10 @@
 
     own = [(is_source, wrap(z + o)) for o in (-2, 2, -1, 1)]
     skipped = []
-    for d in range(3, 14):
-        through = plus if d <= 8 else minus
-        skipped.append((is_source & skips(through, wrap(z + d)), wrap(z + d)))
+    for d in range(9, 14):
+        skipped.append((is_source & skips(minus, wrap(z + d)), wrap(z + d)))
     passed = [
-        ((role == 1 if o == 3 else is_relay) & ~skips(z, wrap(z + o)), wrap(z + o))
+        ((role == 1) | ((role == 3) & ~skips(z, wrap(z + o))) if o != 3 else role == 1, wrap(z + o))
         for o in (3, -2, 2, -1, 1)
     ]
     first = own + skipped
@@ -149,46 +149,63 @@
     def count(pairs, test):
         return sum(jnp.where(applies & test(place), 1, 0) for applies, place in pairs)
 
-    lower = lambda place: place < z
-    higher = lambda place: place > z
+    def tells(place):
+        return (z < place) | (place >= NZ // 2)
+
+    def knows(place):
+        return (place < z) | (z >= NZ // 2)
+
+    def unknown(place):
+        return ~knows(place)
 
     barrier = pltpu.get_barrier_semaphore()
 
-    @pl.when(served & (holder > z))
+    @pl.when(served & tells(holder))
     def _():
         each(0, NY, lambda i: signal(barrier, holders(i)))
 
-    @pl.when(is_relay & (sent > z))
+    @pl.when(is_relay & tells(sent))
     def _():
         signal(barrier, (sent, me))
 
     for applies, place in first + passed:
-        @pl.when(applies & (place > z))
+        @pl.when(applies & tells(place))
         def _(place=place):
             signal(barrier, target(place))
 
     for applies, place in legs:
-        @pl.when(applies & (place > z))
+        @pl.when(applies & tells(place))
         def _(place=place):
             signal(barrier, (place, me))
 
-    each(seat + 1, TEAM, lambda i: signal(barrier, team(i)))
-    each(x + 1, NX, lambda i: signal(barrier, across(i)))
+    each(1, GROUP, lambda i: signal(barrier, (z, lax.rem(me + i, GROUP))))
 
     loads = [
         pltpu.make_async_copy(a, b, load_sem.at[i])
         for i, (a, b) in enumerate((
             (inv_ref, inv_v), (order_ref, order_v), (weight_ref, weight_v), (points_ref, points_v), (noise_ref, noise_out),
+            (pool_ref, pool_v),
         ))
     ]
     for load in loads:
         load.start()
 
+    loads[1].wait()
+    loads[5].wait()
+    pick = jnp.where(
+        lax.broadcasted_iota(jnp.int32, (PANEL, PANEL), 0) == order_v[...], 1.0, 0.0
+    ).astype(BF16)
+    parts = [
+        lax.dot_general(pick, part, (((0,), (0,)), ((), ())), preferred_element_type=F32)
+        for part in split3(pool_v[...])
+    ]
+    mixed[...] = (parts[0] + parts[1]) + parts[2]
+
     expected = (
-        seat + x + count(first + passed + legs, lower)
-        + jnp.where(served & (holder < z), NY, 0) + jnp.where(is_relay & (sent < z), 1, 0)
+        GROUP - 1 + count(first + passed + legs, knows)
+        + jnp.where(served & knows(holder), NY, 0) + jnp.where(is_relay & knows(sent), 1, 0)
     )
-    wait_for(barrier, expected)
+    pl.semaphore_wait(barrier, expected)
 
     own_slice = points_ref.at[pl.ds(pl.multiple_of(core * COLS + y * SLICE, SLICE), SLICE)]
     here = cols.at[pl.ds(pl.multiple_of(y * SLICE, SLICE), SLICE)]
@@ -217,34 +234,29 @@
             def _(number=number, place=place):
                 leg_two(from_ref, place, number).start()
 
-    start_one(lambda number, place: place < z)
-    start_two(first, own_slice, lower)
-
-    each(0, seat, lambda i: signal(ready_near, team(i)))
-    each(0, x, lambda i: signal(ready_near, across(i)))
-
-    @pl.when(is_relay & (sent < z) & (role == 1))
+    start_one(lambda number, place: knows(place) & (place < NZ // 2))
+    start_two(first, own_slice, lambda place: knows(place) & (wrap(place - z + 2) > 4))
+    start_one(lambda number, place: knows(place) & (place >= NZ // 2))
+    start_two(first, own_slice, lambda place: knows(place) & (wrap(place - z + 2) <= 4))
+
+    @pl.when(is_relay & ~tells(sent) & (role == 1))
     def _():
         signal(ready_plus, (sent, me))
 
-    @pl.when(is_relay & (sent < z) & (role == 3))
+    @pl.when(is_relay & ~tells(sent) & (role == 3))
     def _():
         signal(ready_minus, (sent, me))
 
-    @pl.when(served & (holder < z))
+    @pl.when(served & ~tells(holder))
     def _():
         each(0, NY, lambda i: signal(ready_two, holders(i)))
-
-    wait_for(ready_near, (TEAM - 1 - seat) + (NX - 1 - x))
-    others(0, NX, x, lambda i: signal(ready_plane, across(i)))
-    pl.semaphore_wait(ready_plane, NX - 1)
 
     my_rows = pl.ds(pl.multiple_of(me * PIECE, PIECE), PIECE)
 
     def spread(step):
         other = lax.rem(me + step, GROUP)
         pltpu.make_async_remote_copy(
-            src_ref=pool_ref.at[pl.ds(pl.multiple_of(other * PIECE, PIECE), PIECE)], dst_ref=landed.at[me],
+            src_ref=mixed.at[pl.ds(pl.multiple_of(other * PIECE, PIECE), PIECE)], dst_ref=landed.at[me],
             send_sem=b_send.at[0], recv_sem=b_recv.at[0], device_id=(z, other), device_id_type=MESH,
         ).start()
 
@@ -260,56 +272,14 @@
 
     some = chosen.at[pl.ds(0, (GROUP - 1) * PIECE)]
     each(1, GROUP, spread)
-    keep = pltpu.make_async_copy(pool_ref.at[my_rows], landed.at[me], load_sem.at[5])
-    keep.start()
+    landed[me] = mixed[my_rows]
 
     loads[0].wait()
-    loads[1].wait()
-    pick = jnp.where(
-        lax.broadcasted_iota(jnp.int32, (PANEL, PANEL), 0) == order_v[...], 1.0, 0.0
-    ).astype(BF16)
-    inv_high, inv_low = split2(inv_v[...])
-    w_high[...] = dot_nt(inv_high, pick).astype(BF16)
-    w_low[...] = dot_nt(inv_low, pick).astype(BF16)
-
-    @pl.when(is_source & (plus > z))
-    def _():
-        pl.semaphore_wait(ready_plus, 1)
-    start_one(lambda number, place: (place > z) & (number == 0))
+    w_high[...], w_low[...] = split2(inv_v[...])
 
     wait_bytes(some, b_recv.at[0])
-    keep.wait()
     chosen[my_rows] = landed[index_ref[0]]
     each(1, GROUP, share)
-
-    def pass_on():
-        @pl.when(is_source & (minus > z))
-        def _():
-            pl.semaphore_wait(ready_minus, 1)
-        start_one(lambda number, place: (place > z) & (number == 1))
-
-        @pl.when(is_relay)
-        def _():
-            leg_one(plus, 0).wait_recv()
-            start_two(passed, relay, lower)
-
-            @pl.when(line != y)
-            def _():
-                leg_two(relay, z, SAME).start()
-
-            @pl.when(line == y)
-            def _():
-                copy = pltpu.make_async_copy(relay, here, load_sem.at[0])
-                copy.start()
-                copy.wait()
-
-        wait_for(ready_two, count(first + passed, higher))
-        start_two(first, own_slice, higher)
-        start_two(passed, relay, higher)
-
-    @pl.when(z >= NZ // 2)
-    def _():
-        pass_on()
 
     loads[2].wait()
     loads[3].wait()
@@ -326,22 +296,53 @@
         copy.start()
         copy.wait()
 
+    @pl.when(is_source)
+    def _():
+        for number, (place, ready) in enumerate(((plus, ready_plus), (minus, ready_minus))):
+            @pl.when(unknown(place))
+            def _(number=number, place=place, ready=ready):
+                pl.semaphore_wait(ready, 1)
+                leg_one(place, number).start()
+
+        wait_for(ready_two, count(first, unknown))
+        start_two(first, own_slice, unknown)
+
+    @pl.when(is_relay)
+    def _():
+        leg_one(plus, 0).wait_recv()
+        start_two(passed, relay, knows)
+
+        @pl.when(line != y)
+        def _():
+            leg_two(relay, z, SAME).start()
+
+        wait_for(ready_two, count(passed, unknown))
+        start_two(passed, relay, unknown)
+
+        @pl.when(line == y)
+        def _():
+            copy = pltpu.make_async_copy(relay, here, load_sem.at[0])
+            copy.start()
+            copy.wait()
+
     wait_bytes(some, b_recv.at[1])
-
-    @pl.when(z < NZ // 2)
-    def _():
-        pass_on()
 
     pan_pair, pan_kept = scaled_pair(chosen[...], root)
     pan_out[...] = pan_pair
     pan_norm[...] = column_norms(pan_kept)
 
-    @pl.loop(0, ROWS // BLOCK)
-    def _(step):
+    def factor(step, carry):
         rows = pl.ds(pl.multiple_of(step * BLOCK, BLOCK), BLOCK)
         part = split2(kern(pair_out[rows], norm_out[rows, 0:1], pan_out[...], pan_norm[...]))
-        part = split2(triple_nt(part, (w_high[...], w_low[...])))
-        g_high[rows], g_low[rows] = split2(triple_nn(part, (w_high[...], w_low[...])))
+        low, high = pl.ds(0, HALF), pl.ds(HALF, HALF)
+        left = split2(triple_nt([k[:, :HALF] for k in part], (w_high[low, low], w_low[low, low])))
+        right = split2(triple_nt(part, (w_high[high, :], w_low[high, :])))
+        both = [jnp.concatenate(pair, axis=1) for pair in zip(left, right)]
+        g_high[rows, low], g_low[rows, low] = split2(triple_nn(both, (w_high[:, low], w_low[:, low])))
+        g_high[rows, high], g_low[rows, high] = split2(triple_nn(right, (w_high[high, high], w_low[high, high])))
+        return carry
+
+    lax.fori_loop(0, ROWS // BLOCK, factor, 0)
 
     for other in range(NY):
         @pl.when((away != 0) & ~((holder == z) & (other == y)))
@@ -389,6 +390,8 @@
             pltpu.VMEM((ROWS, FEAT), F32),
             pltpu.VMEM((PANEL, PANEL), F32),
             pltpu.VMEM((1, FEAT), F32),
+            pltpu.VMEM((PANEL, FEAT), F32),
+            pltpu.VMEM((PANEL, FEAT), F32),
             pltpu.VMEM((PANEL, PANEL), BF16),
             pltpu.VMEM((PANEL, PANEL), BF16),
             pltpu.VMEM((GROUP, PIECE, FEAT), F32),
@@ -396,7 +399,7 @@
             pltpu.VMEM((SLICE, FEAT), F32),
             pltpu.VMEM((COLS, FEAT), F32),
             dma((6,)),
-            flag, flag, flag, flag, flag,
+            flag, flag, flag,
             dma((2,)),
             dma,
             dma((16,)),
@@ -421,12 +424,12 @@
     side = split2(kern(pair, row_norms(kept), pan_ref[...], pan_norm[...]))
     noise = noise_ref[:, pl.ds(pl.multiple_of(col % 2 * COLS, COLS), COLS)]
     copies = []
-    for step in range(ROWS // BLOCK):
-        rows = pl.ds(step * BLOCK, BLOCK)
+    for step in range(ROWS // TILE):
+        rows = pl.ds(step * TILE, TILE)
         update = triple_nt((g_high[rows], g_low[rows]), side)
         part = kern(pair_ref[rows], norm_ref[rows, 0:1], pair, norms)
-        row_ids = lax.broadcasted_iota(jnp.int32, (BLOCK, COLS), 0) + (step * BLOCK + z * ROWS)
-        col_ids = lax.broadcasted_iota(jnp.int32, (BLOCK, COLS), 1) + col * COLS
+        row_ids = lax.broadcasted_iota(jnp.int32, (TILE, COLS), 0) + (step * TILE + z * ROWS)
+        col_ids = lax.broadcasted_iota(jnp.int32, (TILE, COLS), 1) + col * COLS
         tile[rows] = part + jnp.where(row_ids == col_ids, noise, 0.0) - update
         copy = pltpu.make_async_copy(tile.at[rows], out_ref.at[rows], out_sem.at[step])
         copy.start()
@@ -444,7 +447,7 @@
         out_specs=pl.BlockSpec(memory_space=pltpu.HBM),
         scratch_shapes=[
             pltpu.VMEM((ROWS, COLS), F32),
-            pltpu.SemaphoreType.DMA((ROWS // BLOCK,)),
+            pltpu.SemaphoreType.DMA((ROWS // TILE,)),
         ],
         compiler_params=pltpu.CompilerParams(vmem_limit_bytes=40 * 2**20),
         cost_estimate=pl.CostEstimate(flops=3 * 10**9, bytes_accessed=2**22, transcendentals=2**19),

time: 37 us -> 34.1 us (0.922)
  Pallas kernels: 36 us -> 33.2 us
    pallas_call x1, Pallas kernels: 31.9 us -> 29.1 us  [gather_points(): pl.pallas_call(gather_kernel, out_shape=outs, in_specs=[pl.BlockSpec(memo...]
where the time goes in v3:
time: 34.1 us; the launch traced here: 33.9 us
  Pallas kernels  33.2 us (97%)
  between operations  0.66 us (2%)
    pallas_call x1, Pallas kernels, gather_points(): pl.pallas_call(gather_kernel, out_shape=outs, in_specs=[pl.BlockSpec(memo...  29.1 us
    pallas_call x1, Pallas kernels, make_tile(): pl.pallas_call(tile_kernel, out_shape=jax.ShapeDtypeStruct((ROWS, COLS),...  4.13 us

profile of v3, /device:TPU:1, one launch (start us, length us, event | category | flops | bytes accessed | tf_op | source)
XLA Modules:
  0.0 33.9 jit_solution(9019125358241038607)
XLA Ops:
  0.7 29.1 %gather_points.1 = (f32[512,128]{1,0:T(8,128)S(1)}, bf16[512,256]{1,0:T(8,128)(2,1)S(1)}, f32[1,512]{1,0:T(1,128)S(1)}, bf16[1024,256]{1,0:T(8,128)(2,1)S(1)}, f...) custom-call(s32[1]{0:T(128)S(6)} %copy.8.index_ref, ...), custom_call_target="tpu_custom_call" | custom-call | flops 5000000000 | bytes 4194304 | tf_op jit(solution)/shard_map/gather_points/pallas_call | solution.py:383
  29.8 4.1 %make_tile.1 = f32[1024,512]{1,0:T(8,128)} custom-call(f32[512,128]{1,0:T(8,128)S(1)} %get-tuple-element.14.col_ref, bf16[512,256]{1,0:T(8,128)(2,1)S(1)} %get-tuple-element.15.pan_ref, f32[1,512]{1,0:T(1,128)S(1)} %get-tuple-element.16.pan_norm, bf16[1024,256]{1,0:T(8,128)(2,1)S(1)} %get-tuple-element.17.pair_ref, ...), custom_call_target="tpu_custom_call" | custom-call | flops 3000000000 | bytes 4194304 | tf_op jit(solution)/shard_map/make_tile/pallas_call | solution.py:443

commit v4 on v3

--- a/solution.py
+++ b/solution.py
@@ -159,25 +159,6 @@
         return ~knows(place)
 
     barrier = pltpu.get_barrier_semaphore()
-
-    @pl.when(served & tells(holder))
-    def _():
-        each(0, NY, lambda i: signal(barrier, holders(i)))
-
-    @pl.when(is_relay & tells(sent))
-    def _():
-        signal(barrier, (sent, me))
-
-    for applies, place in first + passed:
-        @pl.when(applies & tells(place))
-        def _(place=place):
-            signal(barrier, target(place))
-
-    for applies, place in legs:
-        @pl.when(applies & tells(place))
-        def _(place=place):
-            signal(barrier, (place, me))
-
     each(1, GROUP, lambda i: signal(barrier, (z, lax.rem(me + i, GROUP))))
 
     loads = [
@@ -189,6 +170,24 @@
     ]
     for load in loads:
         load.start()
+
+    @pl.when(served & tells(holder))
+    def _():
+        each(0, NY, lambda i: signal(barrier, holders(i)))
+
+    @pl.when(is_relay & tells(sent))
+    def _():
+        signal(barrier, (sent, me))
+
+    for applies, place in first + passed:
+        @pl.when(applies & tells(place))
+        def _(place=place):
+            signal(barrier, target(place))
+
+    for applies, place in legs:
+        @pl.when(applies & tells(place))
+        def _(place=place):
+            signal(barrier, (place, me))
 
     loads[1].wait()
     loads[5].wait()
@@ -234,22 +233,27 @@
             def _(number=number, place=place):
                 leg_two(from_ref, place, number).start()
 
-    start_one(lambda number, place: knows(place) & (place < NZ // 2))
-    start_two(first, own_slice, lambda place: knows(place) & (wrap(place - z + 2) > 4))
-    start_one(lambda number, place: knows(place) & (place >= NZ // 2))
-    start_two(first, own_slice, lambda place: knows(place) & (wrap(place - z + 2) <= 4))
-
-    @pl.when(is_relay & ~tells(sent) & (role == 1))
-    def _():
-        signal(ready_plus, (sent, me))
-
-    @pl.when(is_relay & ~tells(sent) & (role == 3))
-    def _():
-        signal(ready_minus, (sent, me))
-
-    @pl.when(served & ~tells(holder))
-    def _():
-        each(0, NY, lambda i: signal(ready_two, holders(i)))
+    def serve():
+        start_one(lambda number, place: knows(place) & (place < NZ // 2))
+        start_two(first, own_slice, lambda place: knows(place) & (wrap(place - z + 2) > 4))
+        start_one(lambda number, place: knows(place) & (place >= NZ // 2))
+        start_two(first, own_slice, lambda place: knows(place) & (wrap(place - z + 2) <= 4))
+
+        @pl.when(is_relay & ~tells(sent) & (role == 1))
+        def _():
+            signal(ready_plus, (sent, me))
+
+        @pl.when(is_relay & ~tells(sent) & (role == 3))
+        def _():
+            signal(ready_minus, (sent, me))
+
+        @pl.when(served & ~tells(holder))
+        def _():
+            each(0, NY, lambda i: signal(ready_two, holders(i)))
+
+    @pl.when(z >= NZ // 2)
+    def _():
+        serve()
 
     my_rows = pl.ds(pl.multiple_of(me * PIECE, PIECE), PIECE)
 
@@ -273,6 +277,11 @@
     some = chosen.at[pl.ds(0, (GROUP - 1) * PIECE)]
     each(1, GROUP, spread)
     landed[me] = mixed[my_rows]
+
+    @pl.when(z < NZ // 2)
+    def _():
+        serve()
+
 
     loads[0].wait()
     w_high[...], w_low[...] = split2(inv_v[...])

time: 34.1 us -> 34 us (level)
  no operation moved by 1% of the time
where the time goes in v4:
time: 34 us; the launch traced here: 33.9 us
  Pallas kernels  33.2 us (98%)
  between operations  0.66 us (2%)
    pallas_call x1, Pallas kernels, gather_points(): pl.pallas_call(gather_kernel, out_shape=outs, in_specs=[pl.BlockSpec(memo...  29.1 us
    pallas_call x1, Pallas kernels, make_tile(): pl.pallas_call(tile_kernel, out_shape=jax.ShapeDtypeStruct((ROWS, COLS),...  4.13 us

profile of v4, /device:TPU:1, one launch (start us, length us, event | category | flops | bytes accessed | tf_op | source)
XLA Modules:
  0.0 33.9 jit_solution(7941631201691430388)
XLA Ops:
  0.7 29.1 %gather_points.1 = (f32[512,128]{1,0:T(8,128)S(1)}, bf16[512,256]{1,0:T(8,128)(2,1)S(1)}, f32[1,512]{1,0:T(1,128)S(1)}, bf16[1024,256]{1,0:T(8,128)(2,1)S(1)}, f...) custom-call(s32[1]{0:T(128)S(6)} %copy.8.index_ref, ...), custom_call_target="tpu_custom_call" | custom-call | flops 5000000000 | bytes 4194304 | tf_op jit(solution)/shard_map/gather_points/pallas_call | solution.py:392
  29.7 4.1 %make_tile.1 = f32[1024,512]{1,0:T(8,128)} custom-call(f32[512,128]{1,0:T(8,128)S(1)} %get-tuple-element.14.col_ref, bf16[512,256]{1,0:T(8,128)(2,1)S(1)} %get-tuple-element.15.pan_ref, f32[1,512]{1,0:T(1,128)S(1)} %get-tuple-element.16.pan_norm, bf16[1024,256]{1,0:T(8,128)(2,1)S(1)} %get-tuple-element.17.pair_ref, ...), custom_call_target="tpu_custom_call" | custom-call | flops 3000000000 | bytes 4194304 | tf_op jit(solution)/shard_map/make_tile/pallas_call | solution.py:452

commit v5 on v3

--- a/solution.py
+++ b/solution.py
@@ -29,7 +29,7 @@
 
 
 def triple_nt(a, b):
-    return dot_nt(a[0], b[0]) + (dot_nt(a[0], b[1]) + dot_nt(a[1], b[0]))
+    return dot_nt(jnp.concatenate([a[0], a[0], a[1]], axis=1), jnp.concatenate([b[0], b[1], b[0]], axis=1))
 
 
 def dot_nn(a, b):
@@ -37,7 +37,7 @@
 
 
 def triple_nn(a, b):
-    return dot_nn(a[0], b[0]) + (dot_nn(a[0], b[1]) + dot_nn(a[1], b[0]))
+    return dot_nn(jnp.concatenate([a[0], a[0], a[1]], axis=1), jnp.concatenate([b[0], b[1], b[0]], axis=0))
 
 
 def split2(x):
@@ -71,8 +71,7 @@
 
 def kern(left, left_norm, right, right_norm):
     high, low = right[:, :FEAT], right[:, FEAT:]
-    cross = dot_nt(left, jnp.concatenate([high, high], axis=1))
-    cross += dot_nt(left, jnp.concatenate([low, low], axis=1))
+    cross = dot_nt(jnp.concatenate([left, left], axis=1), jnp.concatenate([high, high, low, low], axis=1))
     return 2.0 * jnp.exp(cross + left_norm + right_norm)
 
 

time: 34.1 us -> 34 us (level)
  no operation moved by 1% of the time
where the time goes in v5:
time: 34 us; the launch traced here: 33.8 us
  Pallas kernels  33.1 us (97%)
  between operations  0.66 us (2%)
    pallas_call x1, Pallas kernels, gather_points(): pl.pallas_call(gather_kernel, out_shape=outs, in_specs=[pl.BlockSpec(memo...  29 us
    pallas_call x1, Pallas kernels, make_tile(): pl.pallas_call(tile_kernel, out_shape=jax.ShapeDtypeStruct((ROWS, COLS),...  4.11 us

profile of v5, /device:TPU:1, one launch (start us, length us, event | category | flops | bytes accessed | tf_op | source)
XLA Modules:
  0.0 33.8 jit_solution(12881844370727964079)
XLA Ops:
  0.7 29.0 %gather_points.1 = (f32[512,128]{1,0:T(8,128)S(1)}, bf16[512,256]{1,0:T(8,128)(2,1)S(1)}, f32[1,512]{1,0:T(1,128)S(1)}, bf16[1024,256]{1,0:T(8,128)(2,1)S(1)}, f...) custom-call(s32[1]{0:T(128)S(6)} %copy.8.index_ref, ...), custom_call_target="tpu_custom_call" | custom-call | flops 5000000000 | bytes 4194304 | tf_op jit(solution)/shard_map/gather_points/pallas_call | solution.py:382
  29.7 4.1 %make_tile.1 = f32[1024,512]{1,0:T(8,128)} custom-call(f32[512,128]{1,0:T(8,128)S(1)} %get-tuple-element.14.col_ref, bf16[512,256]{1,0:T(8,128)(2,1)S(1)} %get-tuple-element.15.pan_ref, f32[1,512]{1,0:T(1,128)S(1)} %get-tuple-element.16.pan_norm, bf16[1024,256]{1,0:T(8,128)(2,1)S(1)} %get-tuple-element.17.pair_ref, ...), custom_call_target="tpu_custom_call" | custom-call | flops 3000000000 | bytes 4194304 | tf_op jit(solution)/shard_map/make_tile/pallas_call | solution.py:442

commit v6 on v4

--- a/solution.py
+++ b/solution.py
@@ -29,7 +29,7 @@
 
 
 def triple_nt(a, b):
-    return dot_nt(a[0], b[0]) + (dot_nt(a[0], b[1]) + dot_nt(a[1], b[0]))
+    return dot_nt(jnp.concatenate([a[0], a[0], a[1]], axis=1), jnp.concatenate([b[0], b[1], b[0]], axis=1))
 
 
 def dot_nn(a, b):
@@ -37,7 +37,7 @@
 
 
 def triple_nn(a, b):
-    return dot_nn(a[0], b[0]) + (dot_nn(a[0], b[1]) + dot_nn(a[1], b[0]))
+    return dot_nn(jnp.concatenate([a[0], a[0], a[1]], axis=1), jnp.concatenate([b[0], b[1], b[0]], axis=0))
 
 
 def split2(x):
@@ -71,8 +71,7 @@
 
 def kern(left, left_norm, right, right_norm):
     high, low = right[:, :FEAT], right[:, FEAT:]
-    cross = dot_nt(left, jnp.concatenate([high, high], axis=1))
-    cross += dot_nt(left, jnp.concatenate([low, low], axis=1))
+    cross = dot_nt(jnp.concatenate([left, left], axis=1), jnp.concatenate([high, high, low, low], axis=1))
     return 2.0 * jnp.exp(cross + left_norm + right_norm)
 
 

time: 34 us -> 33.9 us (level)
  no operation moved by 1% of the time
where the time goes in v6:
time: 33.9 us; the launch traced here: 33.7 us
  Pallas kernels  33.1 us (98%)
  between operations  0.66 us (2%)
    pallas_call x1, Pallas kernels, gather_points(): pl.pallas_call(gather_kernel, out_shape=outs, in_specs=[pl.BlockSpec(memo...  29 us
    pallas_call x1, Pallas kernels, make_tile(): pl.pallas_call(tile_kernel, out_shape=jax.ShapeDtypeStruct((ROWS, COLS),...  4.11 us

profile of v6, /device:TPU:1, one launch (start us, length us, event | category | flops | bytes accessed | tf_op | source)
XLA Modules:
  0.0 33.7 jit_solution(18370887835644608685)
XLA Ops:
  0.7 29.0 %gather_points.1 = (f32[512,128]{1,0:T(8,128)S(1)}, bf16[512,256]{1,0:T(8,128)(2,1)S(1)}, f32[1,512]{1,0:T(1,128)S(1)}, bf16[1024,256]{1,0:T(8,128)(2,1)S(1)}, f...) custom-call(s32[1]{0:T(128)S(6)} %copy.8.index_ref, ...), custom_call_target="tpu_custom_call" | custom-call | flops 5000000000 | bytes 4194304 | tf_op jit(solution)/shard_map/gather_points/pallas_call | solution.py:391
  29.6 4.1 %make_tile.1 = f32[1024,512]{1,0:T(8,128)} custom-call(f32[512,128]{1,0:T(8,128)S(1)} %get-tuple-element.14.col_ref, bf16[512,256]{1,0:T(8,128)(2,1)S(1)} %get-tuple-element.15.pan_ref, f32[1,512]{1,0:T(1,128)S(1)} %get-tuple-element.16.pan_norm, bf16[1024,256]{1,0:T(8,128)(2,1)S(1)} %get-tuple-element.17.pair_ref, ...), custom_call_target="tpu_custom_call" | custom-call | flops 3000000000 | bytes 4194304 | tf_op jit(solution)/shard_map/make_tile/pallas_call | solution.py:451
